TPU v7x, 512 devices: a whole 4x4x16 slice. The times are simulated.
512 devices in a mesh: band: 4 (over y_lo, core), stn: 128 (over z, y_hi, x).
Axes of the slice: x: 4, y: 4 (y_hi: 2, y_lo: 2; y = y_hi * 2 + y_lo), z: 16, core: 2. Of those that a mesh axis runs over, the one named last changes fastest.
Arguments:
- voltages: bfloat16 [2, 512, 2, 192, 1408], P(None, 'stn', None, 'band'), may hold values from -6 to 6
- station_ok: int32 [512], replicated, may hold values 0 or 1
- delays: int32 [512, 512], replicated, may hold values from 0 to 32767
Outputs:
- beam_power: bfloat16 [512, 3, 36864], P(('band', 'stn'))
All inputs are finite; a program needn't handle non-finite values.
Results may differ from a plain program's by a relative error of at most 0.0061.
Values may be sent and summed in bfloat16 or wider, within the bound.
A program may use at most 128 MiB of HBM per device.

v0:
```python
import math

import jax
import jax.numpy as jnp
from jax import lax
from jax.sharding import PartitionSpec as P

STATIONS = 512
POLS = 2
BEAMS = 512
FINE = 256
TAPS = 4
FRAMES = 3
KEEP = 192
HOP = 192


phase_period = 32768


def prototype():
    length = TAPS * FINE
    sample_index = jnp.arange(length, dtype=jnp.float32)
    centred = (sample_index - (length - 1) / 2.0) / FINE
    window = 0.5 - 0.5 * jnp.cos(2.0 * jnp.pi * (sample_index + 0.5) / length)
    taper = jnp.sinc(centred) * window
    taper = taper / jnp.sqrt(jnp.sum(taper * taper) / FINE)
    return taper.reshape(TAPS, FINE)


def frames_of(samples):
    taper = prototype()
    frame_list = []
    for frame_index in range(FRAMES):
        summed = 0.0
        for tap_index in range(TAPS):
            start = frame_index * HOP + tap_index * FINE
            picked = lax.slice_in_dim(samples, start, start + FINE, 1, samples.ndim - 1)
            summed = summed + picked * taper[tap_index]
        frame_list.append(summed.astype(jnp.bfloat16))
    return jnp.stack(frame_list, axis=3)


def spectrum_table(per_channel):
    sample_index = jnp.arange(FINE, dtype=jnp.int32)
    frequency = (jnp.arange(per_channel, dtype=jnp.int32) - per_channel // 2) % FINE
    turns = sample_index[:, None] * frequency[None, :] % FINE
    phases = 2.0 * jnp.pi * turns.astype(jnp.float32) / FINE
    cosine = jnp.cos(phases) / math.sqrt(FINE)
    sine_part = jnp.sin(phases) / math.sqrt(FINE)
    from_real = jnp.stack([cosine, -sine_part], axis=1)
    from_imag = jnp.stack([sine_part, cosine], axis=1)
    return jnp.stack([from_real, from_imag]).astype(jnp.bfloat16)


def beam_weights(delays, station_ok, channel):
    turns = delays * channel % phase_period
    phases = 2.0 * jnp.pi / phase_period * turns.astype(jnp.float32)
    station_gain = station_ok.astype(jnp.float32) / math.sqrt(STATIONS)
    real_part = (station_gain[:, None] * jnp.cos(phases)).astype(jnp.bfloat16)
    imag_part = (-station_gain[:, None] * jnp.sin(phases)).astype(jnp.bfloat16)
    return jnp.stack(
        [jnp.stack([real_part, imag_part], axis=1), jnp.stack([-imag_part, real_part], axis=1)]
    )


def touched(per_channel, column_count):
    common = math.gcd(per_channel, column_count)
    return -(-(per_channel - common + column_count) // per_channel)


def local(voltages, station_ok, delays):
    band_index = lax.axis_index("band")
    station_rank = lax.axis_index("stn")
    band_count = lax.axis_size("band")
    station_count = lax.axis_size("stn")
    local_stations = voltages.shape[1]
    local_channels = voltages.shape[3]
    per_channel = FINE
    shaped = frames_of(voltages)
    transform = spectrum_table(per_channel)
    spectra = jnp.einsum(
        "rspfcn,rnok->pfosck", shaped, transform, preferred_element_type=jnp.float32
    ).astype(jnp.bfloat16)
    spectra = spectra.reshape(POLS, FRAMES, 2, local_stations, local_channels * per_channel)
    column_count = local_channels * per_channel // station_count
    first_column = station_rank * column_count
    lowest_channel = first_column // per_channel
    owning = (first_column + jnp.arange(column_count, dtype=jnp.int32)) // per_channel
    weights = [
        beam_weights(
            delays, station_ok, band_index * local_channels + lowest_channel + offset_index
        )
        for offset_index in range(touched(per_channel, column_count))
    ]
    received = lax.all_to_all(spectra, "stn", split_axis=4, concat_axis=3, tiled=True)
    powers = None
    for offset_index, weight in enumerate(weights):
        formed = jnp.einsum(
            "rsob,pfrsg->pfobg", weight, received, preferred_element_type=jnp.float32
        )
        detected = jnp.sum(formed * formed, axis=(0, 2))
        if powers is None:
            powers = detected
        else:
            powers = jnp.where(
                (owning == lowest_channel + offset_index)[None, None, :], detected, powers
            )
    powers = powers.astype(jnp.bfloat16)
    beam_share = BEAMS // (band_count * station_count)
    grouped = powers.reshape(FRAMES, band_count, station_count, beam_share, 1, column_count)
    regrouped = lax.all_to_all(
        lax.all_to_all(grouped, "band", split_axis=1, concat_axis=4, tiled=True),
        "stn",
        split_axis=2,
        concat_axis=5,
        tiled=True,
    )
    regrouped = regrouped.reshape(FRAMES, beam_share, band_count * local_channels, per_channel)
    edge = (per_channel - KEEP) // 2
    regrouped = lax.slice_in_dim(regrouped, edge, edge + KEEP, 1, 3)
    regrouped = jnp.transpose(regrouped, (1, 0, 2, 3))
    return regrouped.reshape(beam_share, FRAMES, band_count * local_channels * KEEP)


def solution(mesh):
    placed = (P(None, "stn", None, "band", None), P(), P())
    return jax.shard_map(
        local, mesh=mesh, in_specs=placed, out_specs=P(("band", "stn"), None, None), check_vma=False
    )
```

profile of v0, /device:TPU:1, one launch (start us, length us, event | category | flops | bytes accessed | tf_op | source)
XLA Modules:
  0.0 400.1 jit_solution(14070545289569790007)
XLA Ops:
  0.0 0.7 multiply_reduce_fusion
  0.7 5.0 %fusion.69 = (bf16[2,4,2,48,256]{4,3,2,1,0:T(8,128)(2,1)S(1)}, bf16[2,4,2,48,256]{4,3,2,1,0:T(8,128)(2,1)S(1)}, bf16[2,4,2,48,256]{4,3,2,1,0:T(8,128)(2,1)S(1)},...) fusion(bf16[2,4,2,48,1408]{4,3,2,1,0:T(8,128)(2,1)} %param.3), kind=kLoop, calls=%fused_computation.122 | loop fusion | bytes 9437184 | tf_op jit(solution)/shard_map/slice | solution.py:38
  6.3 0.1 broadcast_divide_fusion
  6.4 1.2 negate_convert_fusion
  7.6 2.1 fusion.24
  9.7 0.8 fusion.8
  10.5 42.9 %copy.87 = bf16[2,3,2,4,48,256]{3,2,1,0,5,4:T(2,128)(2,1)} copy(bf16[2,3,2,4,48,256]{5,4,1,0,3,2:T(8,128)(2,1)S(1)} %fusion.8) | data formatting | bytes 2359296 | tf_op jit(solution)/shard_map/reshape | solution.py:85
  53.4 69.4 %reshape.214 = bf16[128,2,2304]{2,1,0:T(2,128)(2,1)} reshape(bf16[12288,2,3,2,4]{4,3,2,1,0:T(2,128)(2,1)} %bitcast.112) | data formatting | bytes 2359296
  122.9 23.3 %all-to-all-start = ((bf16[128,2,2304]{2,1,0:T(2,128)(2,1)}), bf16[128,2,2304]{2,1,0:T(2,128)(2,1)S(1)}, u32[]{:S(2)}, u32[]{:S(2)}) async-start(bf16[128,2,2304]{2,1,0:T(2,128)(2,1)} %reshape.214), calls=%async_computation | async-start | bytes 2359296 | tf_op jit(solution)/shard_map/all_to_all | solution.py:96
  146.2 0.0 copy-done.4
  146.2 0.0 copy-done
  146.2 8.1 %fusion.20 = (bf16[512,1,512]{2,0,1:T(8,128)(2,1)S(1)}, bf16[512,1,512]{2,0,1:T(8,128)(2,1)S(1)}) fusion(f32[512]{0:T(512)S(1)} %get-tuple-element.39, s32[512,512]{1,0:T(8,128)S(1)} %copy-done, s32[]{:T(128)S(6)} %add.212, s32[]{:T(128)S(6)} %add.211), kind=kLoop, calls=%fused_computation.44 | loop fusion | flops 8388608 | bytes 2099208 | tf_op jit(solution)/shard_map/stack | solution.py:63
  154.3 8.2 %negate_bitcast_fusion.1 = (bf16[512,1,512]{2,0,1:T(8,128)(2,1)S(1)}, bf16[512,512]{1,0:T(8,128)(2,1)S(1)}, bf16[512,1,512]{2,0,1:T(8,128)(2,1)S(1)}, bf16[512,512]{1,0:T(8,128)(2,1)S(1)}) fusion(s32[512,512]{1,0:T(8,128)S(1)} %copy-done, s32[]{:T(128)S(6)} %add.212, f32[512]{0:T(512)S(1)} %get-tuple-element.38, s32[]{:T(128)S(6)} %add.211), kind=kLoop, calls=%fused_computation.50 | loop fusion | flops 9961472 | bytes 3147784 | tf_op jit(solution)/shard_map/stack | solution.py:63
  162.6 1.5 maximum_bitcast_fusion.6
  164.1 1.5 maximum_bitcast_fusion.8
  165.6 37.4 %all-to-all-done = bf16[128,2,2304]{2,1,0:T(2,128)(2,1)S(1)} async-done(((bf16[128,2,2304]{2,1,0:T(2,128)(2,1)}), bf16[128,2,2304]{2,1,0:T(2,128)(2,1)S(1)}, u32[]{:S(2)}, u32[]{:S(2)}) %all-to-all-start) | async-done | bytes 1179680 | tf_op jit(solution)/shard_map/all_to_all | solution.py:96
  203.0 80.3 %reshape.215 = bf16[12288,2,3,2,4]{4,3,2,1,0:T(2,128)(2,1)} reshape(bf16[128,2,2304]{2,1,0:T(2,128)(2,1)S(1)} %all-to-all-done) | data formatting | bytes 2359296
  283.3 64.3 %copy.80 = bf16[2,3,2,4,128,96]{5,4,3,2,1,0:T(8,128)(2,1)S(1)} copy(bf16[2,3,2,4,128,96]{3,2,1,0,5,4:T(2,128)(2,1)} %bitcast.113) | data formatting | bytes 2359296 | tf_op jit(solution)/shard_map/all_to_all | solution.py:96
  347.6 1.2 copy.61
  348.9 0.3 copy-done.2
  349.2 1.4 fusion.1
  350.6 0.1 reduce_sum.38
  350.7 2.7 fusion
  353.3 0.1 reduce_sum.41
  353.4 0.1 fusion.19
  353.5 12.9 %all_to_all.51 = bf16[3,4,128,1,1,96]{2,5,4,3,0,1:T(8,128)(2,1)S(1)} all-to-all(bf16[3,4,128,1,1,96]{2,5,4,3,0,1:T(8,128)(2,1)S(1)} %fusion.19), channel_id=1, replica_groups=mesh['band'=4,'stn'=128] {'band'}, dimensions={1} | all-to-all | bytes 589824 | tf_op jit(solution)/shard_map/all_to_all | solution.py:113
  366.4 0.2 copy.68
  366.6 31.6 %all_to_all.52 = bf16[3,1,128,1,4,96]{5,4,0,3,1,2:T(4,128)(2,1)S(1)} all-to-all(bf16[3,1,128,1,4,96]{5,4,0,3,1,2:T(4,128)(2,1)S(1)} %copy.68), channel_id=1, replica_groups=mesh['band'=4,'stn'=128] {'stn'}, dimensions={2} | all-to-all | bytes 589824 | tf_op jit(solution)/shard_map/all_to_all | solution.py:112
  398.2 0.1 copy.69
  398.3 0.5 reshape.203
  398.8 0.1 slice.80
  399.0 1.1 reshape_transpose.3
  (12 shorter events, 0.1 us)
Async XLA Ops:
  122.9 23.3 %copy-start.4 = (s32[512]{0:T(512)S(1)}, s32[512]{0:T(512)}, u32[]{:S(2)}) copy-start(s32[512]{0:T(512)} %param.4) | copy-start | bytes 6148
  122.9 23.3 %copy-start = (s32[512,512]{1,0:T(8,128)S(1)}, s32[512,512]{1,0:T(8,128)}, u32[]{:S(2)}) copy-start(s32[512,512]{1,0:T(8,128)} %param.5) | copy-start | bytes 3145732
  122.9 80.1 %all-to-all-start = ((bf16[128,2,2304]{2,1,0:T(2,128)(2,1)}), bf16[128,2,2304]{2,1,0:T(2,128)(2,1)S(1)}, u32[]{:S(2)}, u32[]{:S(2)}) async-start(bf16[128,2,2304]{2,1,0:T(2,128)(2,1)} %reshape.214), calls=%async_computation | async-start | bytes 2359296 | tf_op jit(solution)/shard_map/all_to_all | solution.py:96
  347.6 1.3 copy-start.1
  347.6 1.5 copy-start.2
  349.2 1.5 copy-start.3
where the time goes:
time: 407 us; the launch traced here: 400 us
  local copies, waits for them, and re-layouts  266 us (65%)
  blocking collectives  44.5 us (11%)
  waiting for transfers between devices  37.4 us (9%)
  other arithmetic  23.5 us (6%)
  starting transfers between devices  23.3 us (6%)
  matrix products  4.85 us (1%)
    unnamed x12, local copies, waits for them, and re-layouts  150 us
    all_to_all x2, local copies, waits for them, and re-layouts, local(): lax.all_to_all(spectra, 'stn', split_axis=4, concat_axis=3, tiled=True)  65.5 us
    reshape x1, local copies, waits for them, and re-layouts, local(): spectra.reshape(POLS, FRAMES, 2, local_stations, local_channels * per_cha...  42.9 us
    all_to_all x1, waiting for transfers between devices, local(): lax.all_to_all(spectra, 'stn', split_axis=4, concat_axis=3, tiled=True)  37.4 us
    all_to_all x1, blocking collectives, local(): lax.all_to_all(lax.all_to_all(grouped, 'band', split_axis=1, concat_axis=...  31.6 us
    all_to_all x1, starting transfers between devices, local(): lax.all_to_all(spectra, 'stn', split_axis=4, concat_axis=3, tiled=True)  23.3 us
    all_to_all x1, blocking collectives, local(): lax.all_to_all(grouped, 'band', split_axis=1, concat_axis=4, tiled=True)  12.9 us
    another operation x1, other arithmetic, beam_weights(): jnp.stack([-imag_part, real_part], axis=1)  8.25 us
  transfers between devices with their start and end apart: 1, of which 1 were waited for; matrix products, arithmetic and copies ran while one was open for 5% of the time, Pallas kernels for 0%

commit v1 on v0

v1 whole, which is shorter than its diff:
```python
import math

import jax
import jax.numpy as jnp
import numpy as np
from jax import lax
from jax.experimental import pallas as pl
from jax.experimental.pallas import tpu as pltpu
from jax.sharding import PartitionSpec as P

STATIONS = 512
BEAMS = 512
FINE = 256
TAPS = 4
FRAMES = 3
KEEP = 192
HOP = 192
SAMP = 1408
PERIOD = 32768
MESH = pl.DeviceIdType.MESH
VMEM = pltpu.VMEM

BANDS = 4
RINGS = 16
PLANE = 8
STN = RINGS * PLANE
CHANS = 48
PER_Z = CHANS // RINGS
WORKERS = 7
LANES = 128
HALF = 64
ROWS = 2 * STATIONS
DESKS = BANDS * PLANE
SENDERS = RINGS - RINGS // PLANE


def taper_table():
    length = TAPS * FINE
    at = np.arange(length, dtype=np.float64)
    window = 0.5 - 0.5 * np.cos(2.0 * np.pi * (at + 0.5) / length)
    taper = np.sinc((at - (length - 1) / 2.0) / FINE) * window
    taper = taper / np.sqrt(np.sum(taper * taper) / FINE)
    taper = taper.reshape(TAPS, FINE)
    return np.concatenate([taper, np.pad(taper, ((0, 0), (HALF, HALF)))], axis=1).astype(np.float32)


def spectrum_table():
    n = np.arange(FINE)[:, None]
    q = (np.arange(KEEP)[None, :] - KEEP // 2) % FINE
    phase = 2.0 * np.pi * (n * q % FINE) / FINE
    both = np.stack([np.cos(phase), np.sin(phase)], axis=1) / math.sqrt(FINE)
    both = both.reshape(FINE, 2, 3, 1, HALF)
    return np.broadcast_to(both, (FINE, 2, 3, 2, HALF)).reshape(FINE, 768).astype(np.float32)


def sine_coefficients():
    x = np.cos((np.arange(400) + 0.5) * np.pi / 800) * 0.25
    powers = np.stack([x ** (2 * i + 1) for i in range(5)], axis=1)
    return [float(v) for v in np.linalg.lstsq(powers, np.sin(2 * np.pi * x), rcond=None)[0]]


SINE = sine_coefficients()


def one_hot(picked, axis, shape):
    other = lax.broadcasted_iota(jnp.int32, shape, 1 - axis)
    return jnp.where(other == picked(lax.broadcasted_iota(jnp.int32, shape, axis)), 1.0, 0.0).astype(jnp.bfloat16)


def dot(a, b, over=((1,), (0,))):
    return lax.dot_general(a, b, (over, ((), ())), preferred_element_type=jnp.float32)


def kernel(
    volts, taper, waves_far, station_ok, delays, out,
    held, waves, table, filtered, spectra, blocks, middle, landed, delays_in, turns, gains, spread, order, regroup, weights,
    share, share_in, mine, mine_in,
    load_v, load_w, load_d, send_z, recv_z, send_x, recv_x, send_a, recv_a, send_b_sem, recv_b,
):
    band, stn = lax.axis_index("band"), lax.axis_index("stn")
    z, j = stn // PLANE, stn % PLANE
    rank = (j + 3 * PLANE - 1 - z) % PLANE
    works = rank < WORKERS
    at = band * PLANE + j
    bf16, f32 = jnp.bfloat16, jnp.float32

    barrier = pltpu.get_barrier_semaphore()

    def greet_column(i, _):
        other = (band, (z + i) % RINGS * PLANE + j)
        pl.semaphore_signal(barrier, inc=1, device_id=other, device_id_type=MESH)
        return 0

    lax.fori_loop(1, RINGS, greet_column, 0)

    def greet_plane(i, _):
        to = (at + i) % DESKS
        other = (to // PLANE, z * PLANE + to % PLANE)
        pl.semaphore_signal(barrier, inc=1, device_id=other, device_id_type=MESH)
        return 0

    lax.fori_loop(1, DESKS, greet_plane, 0)

    pltpu.make_async_copy(waves_far, waves, load_w).start()
    for s in range(4):
        pltpu.make_async_copy(volts.at[:, s], held.at[:, s], load_v.at[s]).start()
    pltpu.make_async_copy(delays, delays_in, load_d).start()

    low = lax.broadcasted_iota(jnp.int32, (64, 384), 1) % LANES < HALF

    def table_step(i, _):
        at = pl.multiple_of(i * 64, 64)
        cosine, sine = waves[pl.ds(at, 64), :384], waves[pl.ds(at, 64), 384:]
        for p in range(2):
            own = low if p == 0 else jnp.logical_not(low)
            c, s = jnp.where(own, cosine, 0.0), jnp.where(own, sine, 0.0)
            table[pl.ds(512 * p + at, 64), :384] = c.astype(bf16)
            table[pl.ds(512 * p + at, 64), 384:] = (-s).astype(bf16)
            table[pl.ds(512 * p + 256 + at, 64), :384] = s.astype(bf16)
            table[pl.ds(512 * p + 256 + at, 64), 384:] = c.astype(bf16)
        return 0

    pltpu.make_async_copy(waves_far, waves, load_w).wait()
    lax.fori_loop(0, 4, table_step, 0)

    def filter_station(s, _):
        pltpu.make_async_copy(volts.at[:, s], held.at[:, s], load_v.at[s]).wait()

        def filter_step(cb, _):
            for p in range(2):
                for r in range(2):
                    v = held[r, s, p, pl.ds(pl.multiple_of(cb * 16, 16), 16), :].astype(f32)
                    for f in range(FRAMES):
                        total = None
                        for m in range(TAPS):
                            start = f * HOP + m * FINE
                            if f == 1:
                                term = v[:, start - HALF : start + FINE + HALF] * taper[m : m + 1, FINE:]
                            else:
                                term = v[:, start : start + FINE] * taper[m : m + 1, :FINE]
                            total = term if total is None else total + term
                        if f == 1:
                            total = total[:, HALF : HALF + FINE]
                        at = pl.multiple_of((f * 3 + cb) * 64 + s * 16, 16)
                        lanes = slice((p * 2 + r) * FINE, (p * 2 + r + 1) * FINE)
                        filtered[pl.ds(at, 16), lanes] = total.astype(bf16)
            return 0

        lax.fori_loop(0, 3, filter_step, 0)
        return 0

    lax.fori_loop(0, 4, filter_station, 0)

    def transform(f):
        y = dot(filtered[f * 192 : (f + 1) * 192, :], table[...])
        for cb in range(3):
            for s in range(4):
                for part in range(6):
                    ri, g = part // 3, part % 3
                    start = ((f * CHANS + cb * 16) * 3 + g) * 8 + ri * 4 + s
                    spectra[pl.ds(start, 16, stride=24), :] = y[
                        cb * 64 + s * 16 : cb * 64 + s * 16 + 16, part * LANES : (part + 1) * LANES
                    ]

    def pack(t):
        def units(f, zz, first, last):
            start = pl.multiple_of(f * CHANS * 24 + zz * 72 + first * 8, 8)
            return spectra[pl.ds(start, (last - first) * 8), :]

        def pack_step(zz, _):
            if t == 0:
                rows = [units(0, zz, 0, 9), units(1, zz, 0, 5)]
            else:
                rows = [units(1, zz, 5, 9), units(2, zz, 0, 9), jnp.zeros((8, LANES), f32)]
            rows = jnp.concatenate(rows, axis=0).astype(bf16)
            blocks[t, zz] = rows.reshape(WORKERS, 16, LANES)
            return 0

        lax.fori_loop(0, RINGS, pack_step, 0)

    def send_along(t):
        def send_one(slot, zz):
            pltpu.make_async_remote_copy(
                src_ref=blocks.at[t, zz],
                dst_ref=middle.at[t, slot],
                send_sem=send_z,
                recv_sem=recv_z.at[t, slot // 4],
                device_id=(band, zz * PLANE + j),
                device_id_type=MESH,
            ).start()

        def send_two(h, _):
            send_one(2 * h, (z + 1 + h) % RINGS)
            send_one(2 * h + 1, (z + RINGS - 1 - h) % RINGS)
            return 0

        lax.fori_loop(0, RINGS // 2 - 1, send_two, 0)
        send_one(RINGS - 2, (z + RINGS // 2) % RINGS)

    def pass_on(t, k, source, target):
        @pl.when(k == rank)
        def _():
            pltpu.make_async_copy(source, target, recv_x.at[t]).start()

        @pl.when(k != rank)
        def _():
            pltpu.make_async_remote_copy(
                src_ref=source,
                dst_ref=target,
                send_sem=send_x,
                recv_sem=recv_x.at[t],
                device_id=(band, z * PLANE + (z + 1 + k) % PLANE),
                device_id_type=MESH,
            ).start()

    def pass_own(t):
        def one(i, _):
            k = (j + i) % WORKERS
            pass_on(t, k, blocks.at[t, z, k], landed.at[t, j, RINGS - 1])
            return 0

        lax.fori_loop(0, WORKERS, one, 0)

    def pass_group(t, group):
        slots = slice(4 * group, min(4 * group + 4, RINGS - 1))
        slots = pl.ds(slots.start, slots.stop - slots.start)
        arrived = middle.at[t, slots]
        pltpu.make_async_copy(arrived, arrived, recv_z.at[t, group]).wait()

        def one(i, _):
            k = (j + i) % WORKERS
            pass_on(t, k, middle.at[t, slots, k], landed.at[t, j, slots])
            return 0

        lax.fori_loop(0, WORKERS, one, 0)

    transform(0)
    transform(1)
    pack(0)
    pl.semaphore_wait(barrier, RINGS - 1 + DESKS - 1)
    send_along(0)
    pass_own(0)
    transform(2)
    pack(1)
    send_along(1)
    pass_own(1)

    pltpu.make_async_copy(delays, delays_in, load_d).wait()

    def station(k):
        slot = (k >> 3) & 15
        ahead = ((slot >> 1) + 1) * (1 - 2 * (slot & 1))
        ahead = jnp.where(slot == RINGS - 1, 0, ahead)
        return ((((z + RINGS - ahead) & 15) * PLANE) + (k >> 7)) * 4 + (k & 3)

    spread[...] = one_hot(station, 1, (STATIONS, ROWS))
    order[...] = one_hot(lambda b: ((b >> 3) & 3) * 128 + (b >> 5) * 8 + (b & 7), 0, (BEAMS, BEAMS))
    for part in range(2):
        d = delays_in[...]
        d = (d >> 8 if part else d & 255).astype(f32).astype(bf16)
        d = dot(order[...], d, ((1,), (1,))).astype(bf16)
        d = dot(d, spread[...])
        if part:
            turns[...] += d * 256.0
        else:
            turns[...] = d
    ok = jnp.broadcast_to(station_ok[...].astype(f32), (8, STATIONS)).astype(bf16)
    gains[...] = dot(ok, spread[...]) * (1.0 / math.sqrt(STATIONS))

    def place(k):
        after = ((k & 15) + RINGS - 1 - j) & 15
        return jnp.where((after & 7) == 7, -1, (after - (after >> 3)) * DESKS + (k >> 4))

    regroup[...] = one_hot(place, 0, (BEAMS, SENDERS * DESKS))

    imag = (lax.broadcasted_iota(jnp.int32, (16, ROWS), 1) >> 2) & 1
    quarter = imag.astype(f32) * -0.25
    first_channel = (band * CHANS + z * PER_Z).astype(f32)

    def weight_step(i, _):
        rows = pl.ds(pl.multiple_of(i * 16, 16), 16)
        x = turns[rows, :]
        gain = jnp.concatenate([gains[...]] * 2, axis=0)
        for c in range(PER_Z):
            turn = x * ((first_channel + float(c)) * (1.0 / PERIOD)) + quarter
            turn = turn - jnp.floor(turn + 0.5)
            a = 0.25 - jnp.abs(turn)
            square = a * a
            value = SINE[4]
            for coefficient in SINE[3::-1]:
                value = value * square + coefficient
            weights[c, rows, :] = (value * a * gain).astype(bf16)
        return 0

    for group in range(4):
        lax.fori_loop(group * 8, group * 8 + 8, weight_step, 0)
        pass_group(0, group)
    pass_group(1, 0)
    pass_group(1, 1)

    upper = lax.broadcasted_iota(jnp.int32, (1, 8, LANES), 1) < 4
    sign = jnp.where(upper, 1.0, -1.0)
    left = lax.broadcasted_iota(jnp.int32, (BEAMS, LANES), 1) < HALF

    after = (z + RINGS - 1 - j) % RINGS
    slot = after - after // PLANE

    def form(t):
        @pl.when(works)
        def _():
            pltpu.make_async_copy(landed.at[t], landed.at[t], recv_x.at[t]).wait()
            x = landed[t].reshape(STN, 16, LANES).astype(f32)
            powers = []
            for h in range(2):
                unit = 2 * (t * WORKERS + rank) + h
                c = (unit // 3) % 3
                for_real = x[:, 8 * h : 8 * h + 8]
                for_imag = pltpu.roll(for_real, 4, 1) * sign
                both = jnp.concatenate([for_real.reshape(ROWS, LANES), for_imag.reshape(ROWS, LANES)], axis=1)
                y = dot(weights[c], both.astype(bf16))
                y = y[:, :LANES] * y[:, :LANES] + y[:, LANES:] * y[:, LANES:]
                powers.append(y + pltpu.roll(y, HALF, 1))
            y = jnp.where(left, powers[0], powers[1]).astype(bf16)
            share[t] = y.reshape(RINGS, DESKS, LANES)

            def send_a_step(i, _, t=t):
                zz = (z + i) % RINGS
                pltpu.make_async_remote_copy(
                    src_ref=share.at[t, zz],
                    dst_ref=share_in.at[t, slot],
                    send_sem=send_a,
                    recv_sem=recv_a.at[t],
                    device_id=(band, zz * PLANE + j),
                    device_id_type=MESH,
                ).start()
                return 0

            lax.fori_loop(1, RINGS, send_a_step, 0)
            pltpu.make_async_copy(share.at[t, z], share_in.at[t, slot], recv_a.at[t]).start()

    form(0)
    pass_group(1, 2)
    pass_group(1, 3)
    form(1)

    for t in range(2):
        pltpu.make_async_copy(share_in.at[t], share_in.at[t], recv_a.at[t]).wait()
        moved = dot(regroup[...], share_in[t].reshape(SENDERS * DESKS, LANES))
        mine[t] = moved.astype(bf16).reshape(DESKS, RINGS, LANES)

        def send_b(i, t=t):
            to = (at + i) % DESKS
            pltpu.make_async_remote_copy(
                src_ref=mine.at[t, to],
                dst_ref=mine_in.at[t, at],
                send_sem=send_b_sem,
                recv_sem=recv_b.at[t],
                device_id=(to // PLANE, z * PLANE + to % PLANE),
                device_id_type=MESH,
            ).start()

        def send_b_step(n, _, send_b=send_b):
            for i in range(5):
                send_b(5 * n + 1 + i)
            return 0

        lax.fori_loop(0, 6, send_b_step, 0)
        send_b(DESKS - 1)
        pltpu.make_async_copy(mine.at[t, at], mine_in.at[t, at], recv_b.at[t]).start()

    for t in range(2):
        pltpu.make_async_copy(mine_in.at[t], mine_in.at[t], recv_b.at[t]).wait()
    width = PER_Z * KEEP
    row = lax.broadcasted_iota(jnp.int32, (RINGS, LANES), 0)
    for b in range(BANDS):
        wide = []
        for t in range(2):
            turned = [mine_in[t, b * PLANE + place].astype(f32) for place in range(PLANE)]
            for step in (1, 2, 4):
                turned = [
                    jnp.where((row & step) > 0, turned[(i + step) % PLANE], turned[i]) for i in range(PLANE)
                ]
            wide += turned[1:]
        wide = jnp.concatenate(wide, axis=1)
        for f in range(FRAMES):
            out[f, b] = wide[:, f * width : (f + 1) * width].astype(bf16)

    some = mine.at[:, pl.ds(0, DESKS - 1)]
    pltpu.make_async_copy(some, some, send_b_sem).wait()
    some = blocks.at[:, pl.ds(0, RINGS - 1)]
    pltpu.make_async_copy(some, some, send_z).wait()

    @pl.when(works)
    def _():
        some = blocks.at[:, :, pl.ds(0, WORKERS - 1)]
        pltpu.make_async_copy(some, some, send_x).wait()
        some = share.at[:, pl.ds(0, RINGS - 1)]
        pltpu.make_async_copy(some, some, send_a).wait()

    @pl.when(jnp.logical_not(works))
    def _():
        pltpu.make_async_copy(blocks, blocks, send_x).wait()


def local(voltages, station_ok, delays):
    in_vmem, anywhere = pl.BlockSpec(memory_space=VMEM), pl.BlockSpec(memory_space=pl.ANY)
    bf16, f32 = jnp.bfloat16, jnp.float32
    dma = pltpu.SemaphoreType.DMA
    formed = pl.pallas_call(
        kernel,
        name="beams",
        out_shape=jax.ShapeDtypeStruct((FRAMES, BANDS, RINGS, PER_Z * KEEP), bf16),
        in_specs=[anywhere, in_vmem, anywhere, in_vmem, anywhere],
        out_specs=in_vmem,
        scratch_shapes=[
            VMEM((2, 4, 2, CHANS, SAMP), bf16),
            VMEM((FINE, 768), f32),
            VMEM((1024, 768), bf16),
            VMEM((FRAMES * CHANS * 4, 1024), bf16),
            VMEM((FRAMES * CHANS * 24, LANES), f32),
            VMEM((2, RINGS, WORKERS, 16, LANES), bf16),
            VMEM((2, RINGS - 1, WORKERS, 16, LANES), bf16),
            VMEM((2, PLANE, RINGS, 16, LANES), bf16),
            VMEM((STATIONS, BEAMS), jnp.int32),
            VMEM((BEAMS, ROWS), f32),
            VMEM((8, ROWS), f32),
            VMEM((STATIONS, ROWS), bf16),
            VMEM((BEAMS, BEAMS), bf16),
            VMEM((BEAMS, SENDERS * DESKS), bf16),
            VMEM((PER_Z, BEAMS, ROWS), bf16),
            VMEM((2, RINGS, DESKS, LANES), bf16),
            VMEM((2, SENDERS, DESKS, LANES), bf16),
            VMEM((2, DESKS, RINGS, LANES), bf16),
            VMEM((2, DESKS, RINGS, LANES), bf16),
            dma((4,)), dma, dma, dma, dma((2, 4)), dma, dma((2,)), dma, dma((2,)), dma, dma((2,)),
        ],
        compiler_params=pltpu.CompilerParams(
            collective_id=0, has_side_effects=True, vmem_limit_bytes=60 * 2**20
        ),
    )(voltages, jnp.asarray(taper_table()), jnp.asarray(spectrum_table()), station_ok.reshape(1, STATIONS), delays)
    return formed.reshape(1, FRAMES, BANDS * CHANS * KEEP)


def solution(mesh):
    placed = (P(None, "stn", None, "band", None), P(), P())
    return jax.shard_map(
        local, mesh=mesh, in_specs=placed, out_specs=P(("band", "stn"), None, None), check_vma=False
    )
```

time: 407 us -> 88.1 us (0.22); the launches traced: 400 us -> 87.9 us
  local copies, waits for them, and re-layouts: 266 us -> 1.99 us
  Pallas kernels: 0 us -> 85.9 us
  blocking collectives: 44.5 us -> 0 us
  waiting for transfers between devices: 37.4 us -> 0 us
  other arithmetic: 23.5 us -> 0 us
  starting transfers between devices: 23.3 us -> 0 us
  matrix products: 4.85 us -> 0 us
    unnamed x12 -> x0, local copies, waits for them, and re-layouts: 150 us -> none
    pallas_call x0 -> x1, Pallas kernels: none -> 85.9 us  [local(): pl.pallas_call(kernel, name='beams', out_shape=jax.ShapeDtypeStruct((FRAM...]
    all_to_all x4 -> x0, local copies, waits for them, and re-layouts: 65.8 us -> none  [the longest x2 65.5 us: local(): lax.all_to_all(spectra, 'stn', split_axis=4, concat_axis=3, tiled=True)]
    all_to_all x2 -> x0, blocking collectives: 44.5 us -> none  [the longest x1 31.6 us: local(): lax.all_to_all(lax.all_to_all(grouped, 'band', split_axis=1, concat_axis=...]
    reshape x2 -> x1, local copies, waits for them, and re-layouts: 43.4 us -> 1.99 us  [local(): return formed.reshape(1, FRAMES, BANDS * CHANS * KEEP)]
    all_to_all x1 -> x0, waiting for transfers between devices: 37.4 us -> none  [local(): lax.all_to_all(spectra, 'stn', split_axis=4, concat_axis=3, tiled=True)]
    all_to_all x1 -> x0, starting transfers between devices: 23.3 us -> none  [local(): lax.all_to_all(spectra, 'stn', split_axis=4, concat_axis=3, tiled=True)]
    another operation x7 -> x0, other arithmetic: 22.7 us -> none  [the longest x1 8.25 us: beam_weights(): jnp.stack([-imag_part, real_part], axis=1)]
  transfers between devices with their start and end apart: 1 -> 0, of which waited for: 1 -> 0; matrix products, arithmetic and copies ran while one was open for 5% -> 0% of each run, Pallas kernels for 0% -> 0%
where the time goes in v1:
time: 88.1 us; the launch traced here: 87.9 us
  Pallas kernels  85.9 us (98%)
  local copies, waits for them, and re-layouts  1.99 us (2%)
    pallas_call x1, Pallas kernels, local(): pl.pallas_call(kernel, name='beams', out_shape=jax.ShapeDtypeStruct((FRAM...  85.9 us
    reshape x1, local copies, waits for them, and re-layouts, local(): return formed.reshape(1, FRAMES, BANDS * CHANS * KEEP)  1.99 us

profile of v1, /device:TPU:1, one launch (start us, length us, event | category | flops | bytes accessed | tf_op | source)
XLA Modules:
  0.0 87.9 jit_solution(6335635014988597232)
XLA Ops:
  0.0 85.9 %beams.1 = bf16[3,4,16,576]{3,2,1,0:T(8,128)(2,1)} custom-call(bf16[2,4,2,48,1408]{4,3,2,1,0:T(8,128)(2,1)} %volts.1, f32[4,640]{1,0:T(4,128)} %constant.4.clone.taper, f32[256,768]{1,0:T(8,128)} %constant.5.clone.waves_far, s32[1,512]{1,0:T(1,128)} %bitcast.3, s32[512,512]{1,0:T(8,128)} %delays.1), custom_call_target="tpu_custom_call" | custom-call | tf_op jit(solution)/shard_map/beams/pallas_call | solution.py:409
  85.9 2.0 %reshape.7 = bf16[1,3,36864]{2,1,0:T(4,128)(2,1)} reshape(bf16[3,4,16,576]{3,2,1,0:T(8,128)(2,1)} %beams.1) | data formatting | bytes 442368 | tf_op jit(solution)/shard_map/reshape | solution.py:441

commit v2 on v1

--- a/solution.py
+++ b/solution.py
@@ -73,9 +73,9 @@
 
 def kernel(
     volts, taper, waves_far, station_ok, delays, out,
-    held, waves, table, filtered, spectra, blocks, middle, landed, delays_in, turns, gains, spread, order, regroup, weights,
+    held, waves, table, filtered, spectra, blocks, middle, relay, landed, delays_in, turns, gains, spread, order, regroup, weights,
     share, share_in, mine, mine_in,
-    load_v, load_w, load_d, send_z, recv_z, send_x, recv_x, send_a, recv_a, send_b_sem, recv_b,
+    load_v, load_w, load_d, send_z, recv_z, relay_in, relay_out, send_x, recv_x, send_a, recv_a, send_b_sem, recv_b,
 ):
     band, stn = lax.axis_index("band"), lax.axis_index("stn")
     z, j = stn // PLANE, stn % PLANE
@@ -194,8 +194,28 @@
             send_one(2 * h + 1, (z + RINGS - 1 - h) % RINGS)
             return 0
 
+        pltpu.make_async_remote_copy(
+            src_ref=blocks.at[t, (z + RINGS // 2) % RINGS],
+            dst_ref=relay.at[t],
+            send_sem=send_z,
+            recv_sem=relay_in.at[t],
+            device_id=(band, (z + quarter_way[t]) % RINGS * PLANE + j),
+            device_id_type=MESH,
+        ).start()
         lax.fori_loop(0, RINGS // 2 - 1, send_two, 0)
-        send_one(RINGS - 2, (z + RINGS // 2) % RINGS)
+
+    quarter_way = (RINGS // 4, RINGS - RINGS // 4)
+
+    def second_leg(t):
+        pltpu.make_async_copy(relay.at[t], relay.at[t], relay_in.at[t]).wait()
+        pltpu.make_async_remote_copy(
+            src_ref=relay.at[t],
+            dst_ref=middle.at[t, RINGS - 2],
+            send_sem=relay_out,
+            recv_sem=recv_z.at[t, 3],
+            device_id=(band, (z + quarter_way[t]) % RINGS * PLANE + j),
+            device_id_type=MESH,
+        ).start()
 
     def pass_on(t, k, source, target):
         @pl.when(k == rank)
@@ -294,7 +314,10 @@
 
     for group in range(4):
         lax.fori_loop(group * 8, group * 8 + 8, weight_step, 0)
+        if group == 0:
+            second_leg(0)
         pass_group(0, group)
+    second_leg(1)
     pass_group(1, 0)
     pass_group(1, 1)
 
@@ -387,6 +410,7 @@
 
     some = mine.at[:, pl.ds(0, DESKS - 1)]
     pltpu.make_async_copy(some, some, send_b_sem).wait()
+    pltpu.make_async_copy(relay, relay, relay_out).wait()
     some = blocks.at[:, pl.ds(0, RINGS - 1)]
     pltpu.make_async_copy(some, some, send_z).wait()
 
@@ -403,7 +427,7 @@
 
 
 def local(voltages, station_ok, delays):
-    in_vmem, anywhere = pl.BlockSpec(memory_space=VMEM), pl.BlockSpec(memory_space=pl.ANY)
+    in_vmem, anywhere = pl.BlockSpec(memory_space=VMEM), pl.BlockSpec(memory_space=pltpu.HBM)
     bf16, f32 = jnp.bfloat16, jnp.float32
     dma = pltpu.SemaphoreType.DMA
     formed = pl.pallas_call(
@@ -420,6 +444,7 @@
             VMEM((FRAMES * CHANS * 24, LANES), f32),
             VMEM((2, RINGS, WORKERS, 16, LANES), bf16),
             VMEM((2, RINGS - 1, WORKERS, 16, LANES), bf16),
+            VMEM((2, WORKERS, 16, LANES), bf16),
             VMEM((2, PLANE, RINGS, 16, LANES), bf16),
             VMEM((STATIONS, BEAMS), jnp.int32),
             VMEM((BEAMS, ROWS), f32),
@@ -432,7 +457,7 @@
             VMEM((2, SENDERS, DESKS, LANES), bf16),
             VMEM((2, DESKS, RINGS, LANES), bf16),
             VMEM((2, DESKS, RINGS, LANES), bf16),
-            dma((4,)), dma, dma, dma, dma((2, 4)), dma, dma((2,)), dma, dma((2,)), dma, dma((2,)),
+            dma((4,)), dma, dma, dma, dma((2, 4)), dma((2,)), dma, dma, dma((2,)), dma, dma((2,)), dma, dma((2,)),
         ],
         compiler_params=pltpu.CompilerParams(
             collective_id=0, has_side_effects=True, vmem_limit_bytes=60 * 2**20

time: 88.1 us -> 89.3 us (1.014)
  Pallas kernels: 85.9 us -> 87.1 us
    pallas_call x1, Pallas kernels: 85.9 us -> 87.1 us  [local(): pl.pallas_call(kernel, name='beams', out_shape=jax.ShapeDtypeStruct((FRAM...]
where the time goes in v2:
time: 89.3 us; the launch traced here: 89.1 us
  Pallas kernels  87.1 us (98%)
  local copies, waits for them, and re-layouts  1.99 us (2%)
    pallas_call x1, Pallas kernels, local(): pl.pallas_call(kernel, name='beams', out_shape=jax.ShapeDtypeStruct((FRAM...  87.1 us
    reshape x1, local copies, waits for them, and re-layouts, local(): return formed.reshape(1, FRAMES, BANDS * CHANS * KEEP)  1.99 us

profile of v2, /device:TPU:1, one launch (start us, length us, event | category | flops | bytes accessed | tf_op | source)
XLA Modules:
  0.0 89.1 jit_solution(15421477571169779653)
XLA Ops:
  0.0 87.1 %beams.1 = bf16[3,4,16,576]{3,2,1,0:T(8,128)(2,1)} custom-call(bf16[2,4,2,48,1408]{4,3,2,1,0:T(8,128)(2,1)} %volts.1, f32[4,640]{1,0:T(4,128)} %constant.4.clone.taper, f32[256,768]{1,0:T(8,128)} %constant.5.clone.waves_far, s32[1,512]{1,0:T(1,128)} %bitcast.3, s32[512,512]{1,0:T(8,128)} %delays.1), custom_call_target="tpu_custom_call" | custom-call | tf_op jit(solution)/shard_map/beams/pallas_call | solution.py:433
  87.1 2.0 %reshape.7 = bf16[1,3,36864]{2,1,0:T(4,128)(2,1)} reshape(bf16[3,4,16,576]{3,2,1,0:T(8,128)(2,1)} %beams.1) | data formatting | bytes 442368 | tf_op jit(solution)/shard_map/reshape | solution.py:466

commit v3 on v1

--- a/solution.py
+++ b/solution.py
@@ -64,7 +64,10 @@
 
 def one_hot(picked, axis, shape):
     other = lax.broadcasted_iota(jnp.int32, shape, 1 - axis)
-    return jnp.where(other == picked(lax.broadcasted_iota(jnp.int32, shape, axis)), 1.0, 0.0).astype(jnp.bfloat16)
+    narrow = (8, shape[1]) if axis else (shape[0], LANES)
+    picks = picked(lax.broadcasted_iota(jnp.int32, narrow, axis))
+    picks = jnp.concatenate([picks] * (shape[1 - axis] // narrow[1 - axis]), axis=1 - axis)
+    return jnp.where(other == picks, 1.0, 0.0).astype(jnp.bfloat16)
 
 
 def dot(a, b, over=((1,), (0,))):
@@ -73,7 +76,7 @@
 
 def kernel(
     volts, taper, waves_far, station_ok, delays, out,
-    held, waves, table, filtered, spectra, blocks, middle, landed, delays_in, turns, gains, spread, order, regroup, weights,
+    held, waves, table, filtered, spectra, blocks, middle, landed, delays_in, turns, gains, spread, order, regroup, weights, formed, ordered,
     share, share_in, mine, mine_in,
     load_v, load_w, load_d, send_z, recv_z, send_x, recv_x, send_a, recv_a, send_b_sem, recv_b,
 ):
@@ -179,28 +182,28 @@
         lax.fori_loop(0, RINGS, pack_step, 0)
 
     def send_along(t):
-        def send_one(slot, zz):
+        def send_one(slot, group, zz):
             pltpu.make_async_remote_copy(
                 src_ref=blocks.at[t, zz],
                 dst_ref=middle.at[t, slot],
                 send_sem=send_z,
-                recv_sem=recv_z.at[t, slot // 4],
+                recv_sem=recv_z.at[t, group],
                 device_id=(band, zz * PLANE + j),
                 device_id_type=MESH,
             ).start()
 
         def send_two(h, _):
-            send_one(2 * h, (z + 1 + h) % RINGS)
-            send_one(2 * h + 1, (z + RINGS - 1 - h) % RINGS)
+            for way in ((band + 0) % 2, (band + 1) % 2):
+                send_one(2 * h + way, h // 2, (z + (1 + h) * (1 - 2 * way) + RINGS) % RINGS)
             return 0
 
         lax.fori_loop(0, RINGS // 2 - 1, send_two, 0)
-        send_one(RINGS - 2, (z + RINGS // 2) % RINGS)
-
-    def pass_on(t, k, source, target):
+        send_one(RINGS - 2, 3, (z + RINGS // 2) % RINGS)
+
+    def pass_on(t, group, k, source, target):
         @pl.when(k == rank)
         def _():
-            pltpu.make_async_copy(source, target, recv_x.at[t]).start()
+            pltpu.make_async_copy(source, target, recv_x.at[t, group]).start()
 
         @pl.when(k != rank)
         def _():
@@ -208,7 +211,7 @@
                 src_ref=source,
                 dst_ref=target,
                 send_sem=send_x,
-                recv_sem=recv_x.at[t],
+                recv_sem=recv_x.at[t, group],
                 device_id=(band, z * PLANE + (z + 1 + k) % PLANE),
                 device_id_type=MESH,
             ).start()
@@ -216,20 +219,20 @@
     def pass_own(t):
         def one(i, _):
             k = (j + i) % WORKERS
-            pass_on(t, k, blocks.at[t, z, k], landed.at[t, j, RINGS - 1])
+            pass_on(t, 3, k, blocks.at[t, z, k], landed.at[t, 3, j, 3])
             return 0
 
         lax.fori_loop(0, WORKERS, one, 0)
 
     def pass_group(t, group):
-        slots = slice(4 * group, min(4 * group + 4, RINGS - 1))
-        slots = pl.ds(slots.start, slots.stop - slots.start)
+        count = 3 if group == 3 else 4
+        slots = pl.ds(4 * group, count)
         arrived = middle.at[t, slots]
         pltpu.make_async_copy(arrived, arrived, recv_z.at[t, group]).wait()
 
         def one(i, _):
             k = (j + i) % WORKERS
-            pass_on(t, k, middle.at[t, slots, k], landed.at[t, j, slots])
+            pass_on(t, group, k, middle.at[t, slots, k], landed.at[t, group, j, pl.ds(0, count)])
             return 0
 
         lax.fori_loop(0, WORKERS, one, 0)
@@ -248,22 +251,17 @@
     pltpu.make_async_copy(delays, delays_in, load_d).wait()
 
     def station(k):
-        slot = (k >> 3) & 15
+        slot = (k >> 8) * 4 + ((k >> 3) & 3)
         ahead = ((slot >> 1) + 1) * (1 - 2 * (slot & 1))
         ahead = jnp.where(slot == RINGS - 1, 0, ahead)
-        return ((((z + RINGS - ahead) & 15) * PLANE) + (k >> 7)) * 4 + (k & 3)
+        return ((((z + RINGS - ahead) & 15) * PLANE) + ((k >> 5) & 7)) * 4 + (k & 3)
 
     spread[...] = one_hot(station, 1, (STATIONS, ROWS))
     order[...] = one_hot(lambda b: ((b >> 3) & 3) * 128 + (b >> 5) * 8 + (b & 7), 0, (BEAMS, BEAMS))
-    for part in range(2):
-        d = delays_in[...]
-        d = (d >> 8 if part else d & 255).astype(f32).astype(bf16)
-        d = dot(order[...], d, ((1,), (1,))).astype(bf16)
-        d = dot(d, spread[...])
-        if part:
-            turns[...] += d * 256.0
-        else:
-            turns[...] = d
+    d = delays_in[...]
+    d = jnp.concatenate([d >> 8, d & 255], axis=0).astype(f32).astype(bf16)
+    d = dot(order[...], d, ((1,), (1,))).astype(bf16)
+    turns[...] = dot(d[:, :STATIONS], spread[...]) * 256.0 + dot(d[:, STATIONS:], spread[...])
     ok = jnp.broadcast_to(station_ok[...].astype(f32), (8, STATIONS)).astype(bf16)
     gains[...] = dot(ok, spread[...]) * (1.0 / math.sqrt(STATIONS))
 
@@ -271,7 +269,7 @@
         after = ((k & 15) + RINGS - 1 - j) & 15
         return jnp.where((after & 7) == 7, -1, (after - (after >> 3)) * DESKS + (k >> 4))
 
-    regroup[...] = one_hot(place, 0, (BEAMS, SENDERS * DESKS))
+    regroup[...] = one_hot(place, 0, (BEAMS, BEAMS))[:, : SENDERS * DESKS]
 
     imag = (lax.broadcasted_iota(jnp.int32, (16, ROWS), 1) >> 2) & 1
     quarter = imag.astype(f32) * -0.25
@@ -305,19 +303,31 @@
     after = (z + RINGS - 1 - j) % RINGS
     slot = after - after // PLANE
 
+    def channel_of(t, h):
+        return ((2 * (t * WORKERS + rank) + h) // 3) % 3
+
+    def gather(t, group):
+        @pl.when(works)
+        def _():
+            pltpu.make_async_copy(landed.at[t, group], landed.at[t, group], recv_x.at[t, group]).wait()
+            x = landed[t, group].reshape(ROWS // 32, 16, LANES).astype(f32)
+            for h in range(2):
+                for_real = x[:, 8 * h : 8 * h + 8]
+                for_imag = pltpu.roll(for_real, 4, 1) * sign
+                both = [for_real.reshape(ROWS // 4, LANES), for_imag.reshape(ROWS // 4, LANES)]
+                both = jnp.concatenate(both, axis=1).astype(bf16)
+                y = dot(weights[channel_of(t, h), :, group * 256 : group * 256 + 256], both)
+                if group == 0:
+                    formed[h] = y
+                else:
+                    formed[h] += y
+
     def form(t):
         @pl.when(works)
         def _():
-            pltpu.make_async_copy(landed.at[t], landed.at[t], recv_x.at[t]).wait()
-            x = landed[t].reshape(STN, 16, LANES).astype(f32)
             powers = []
             for h in range(2):
-                unit = 2 * (t * WORKERS + rank) + h
-                c = (unit // 3) % 3
-                for_real = x[:, 8 * h : 8 * h + 8]
-                for_imag = pltpu.roll(for_real, 4, 1) * sign
-                both = jnp.concatenate([for_real.reshape(ROWS, LANES), for_imag.reshape(ROWS, LANES)], axis=1)
-                y = dot(weights[c], both.astype(bf16))
+                y = formed[h]
                 y = y[:, :LANES] * y[:, :LANES] + y[:, LANES:] * y[:, LANES:]
                 powers.append(y + pltpu.roll(y, HALF, 1))
             y = jnp.where(left, powers[0], powers[1]).astype(bf16)
@@ -338,9 +348,15 @@
             lax.fori_loop(1, RINGS, send_a_step, 0)
             pltpu.make_async_copy(share.at[t, z], share_in.at[t, slot], recv_a.at[t]).start()
 
+    for group in range(4):
+        gather(0, group)
     form(0)
     pass_group(1, 2)
+    gather(1, 0)
+    gather(1, 1)
     pass_group(1, 3)
+    gather(1, 2)
+    gather(1, 3)
     form(1)
 
     for t in range(2):
@@ -368,20 +384,21 @@
         send_b(DESKS - 1)
         pltpu.make_async_copy(mine.at[t, at], mine_in.at[t, at], recv_b.at[t]).start()
 
-    for t in range(2):
-        pltpu.make_async_copy(mine_in.at[t], mine_in.at[t], recv_b.at[t]).wait()
     width = PER_Z * KEEP
     row = lax.broadcasted_iota(jnp.int32, (RINGS, LANES), 0)
+
+    def in_order(t, b):
+        turned = [mine_in[t, b * PLANE + place].astype(f32) for place in range(PLANE)]
+        for step in (1, 2, 4):
+            turned = [jnp.where((row & step) > 0, turned[(i + step) % PLANE], turned[i]) for i in range(PLANE)]
+        return jnp.concatenate(turned[1:], axis=1)
+
+    pltpu.make_async_copy(mine_in.at[0], mine_in.at[0], recv_b.at[0]).wait()
     for b in range(BANDS):
-        wide = []
-        for t in range(2):
-            turned = [mine_in[t, b * PLANE + place].astype(f32) for place in range(PLANE)]
-            for step in (1, 2, 4):
-                turned = [
-                    jnp.where((row & step) > 0, turned[(i + step) % PLANE], turned[i]) for i in range(PLANE)
-                ]
-            wide += turned[1:]
-        wide = jnp.concatenate(wide, axis=1)
+        ordered[b] = in_order(0, b)
+    pltpu.make_async_copy(mine_in.at[1], mine_in.at[1], recv_b.at[1]).wait()
+    for b in range(BANDS):
+        wide = jnp.concatenate([ordered[b], in_order(1, b)], axis=1)
         for f in range(FRAMES):
             out[f, b] = wide[:, f * width : (f + 1) * width].astype(bf16)
 
@@ -420,7 +437,7 @@
             VMEM((FRAMES * CHANS * 24, LANES), f32),
             VMEM((2, RINGS, WORKERS, 16, LANES), bf16),
             VMEM((2, RINGS - 1, WORKERS, 16, LANES), bf16),
-            VMEM((2, PLANE, RINGS, 16, LANES), bf16),
+            VMEM((2, 4, PLANE, 4, 16, LANES), bf16),
             VMEM((STATIONS, BEAMS), jnp.int32),
             VMEM((BEAMS, ROWS), f32),
             VMEM((8, ROWS), f32),
@@ -428,11 +445,13 @@
             VMEM((BEAMS, BEAMS), bf16),
             VMEM((BEAMS, SENDERS * DESKS), bf16),
             VMEM((PER_Z, BEAMS, ROWS), bf16),
+            VMEM((2, BEAMS, 2 * LANES), f32),
+            VMEM((BANDS, RINGS, WORKERS * LANES), f32),
             VMEM((2, RINGS, DESKS, LANES), bf16),
             VMEM((2, SENDERS, DESKS, LANES), bf16),
             VMEM((2, DESKS, RINGS, LANES), bf16),
             VMEM((2, DESKS, RINGS, LANES), bf16),
-            dma((4,)), dma, dma, dma, dma((2, 4)), dma, dma((2,)), dma, dma((2,)), dma, dma((2,)),
+            dma((4,)), dma, dma, dma, dma((2, 4)), dma, dma((2, 4)), dma, dma((2,)), dma, dma((2,)),
         ],
         compiler_params=pltpu.CompilerParams(
             collective_id=0, has_side_effects=True, vmem_limit_bytes=60 * 2**20

time: 88.1 us -> 87.6 us (level)
  no operation moved by 1% of the time
where the time goes in v3:
time: 87.6 us; the launch traced here: 87.4 us
  Pallas kernels  85.4 us (97%)
  local copies, waits for them, and re-layouts  1.99 us (2%)
    pallas_call x1, Pallas kernels, local(): pl.pallas_call(kernel, name='beams', out_shape=jax.ShapeDtypeStruct((FRAM...  85.4 us
    reshape x1, local copies, waits for them, and re-layouts, local(): return formed.reshape(1, FRAMES, BANDS * CHANS * KEEP)  1.99 us

profile of v3, /device:TPU:1, one launch (start us, length us, event | category | flops | bytes accessed | tf_op | source)
XLA Modules:
  0.0 87.4 jit_solution(5474723566777397473)
XLA Ops:
  0.0 85.4 %beams.1 = bf16[3,4,16,576]{3,2,1,0:T(8,128)(2,1)} custom-call(bf16[2,4,2,48,1408]{4,3,2,1,0:T(8,128)(2,1)} %volts.1, f32[4,640]{1,0:T(4,128)} %constant.4.clone.taper, f32[256,768]{1,0:T(8,128)} %constant.5.clone.waves_far, s32[1,512]{1,0:T(1,128)} %bitcast.3, s32[512,512]{1,0:T(8,128)} %delays.1), custom_call_target="tpu_custom_call" | custom-call | tf_op jit(solution)/shard_map/beams/pallas_call | solution.py:426
  85.4 2.0 %reshape.7 = bf16[1,3,36864]{2,1,0:T(4,128)(2,1)} reshape(bf16[3,4,16,576]{3,2,1,0:T(8,128)(2,1)} %beams.1) | data formatting | bytes 442368 | tf_op jit(solution)/shard_map/reshape | solution.py:460

commit v4 on v3

--- a/solution.py
+++ b/solution.py
@@ -68,6 +68,10 @@
     picks = picked(lax.broadcasted_iota(jnp.int32, narrow, axis))
     picks = jnp.concatenate([picks] * (shape[1 - axis] // narrow[1 - axis]), axis=1 - axis)
     return jnp.where(other == picks, 1.0, 0.0).astype(jnp.bfloat16)
+
+
+def distance(h):
+    return (1 + h // 2) * (1 - h % 2) + (RINGS // 2 - 1 - h // 2) * (h % 2)
 
 
 def dot(a, b, over=((1,), (0,))):
@@ -193,8 +197,8 @@
             ).start()
 
         def send_two(h, _):
-            for way in ((band + 0) % 2, (band + 1) % 2):
-                send_one(2 * h + way, h // 2, (z + (1 + h) * (1 - 2 * way) + RINGS) % RINGS)
+            for way in (band % 2, (band + 1) % 2):
+                send_one(2 * h + way, h // 2, (z + distance(h) * (1 - 2 * way) + RINGS) % RINGS)
             return 0
 
         lax.fori_loop(0, RINGS // 2 - 1, send_two, 0)
@@ -252,8 +256,9 @@
 
     def station(k):
         slot = (k >> 8) * 4 + ((k >> 3) & 3)
-        ahead = ((slot >> 1) + 1) * (1 - 2 * (slot & 1))
-        ahead = jnp.where(slot == RINGS - 1, 0, ahead)
+        pair = slot >> 1
+        ahead = jnp.where((pair & 1) == 0, 1 + (pair >> 1), RINGS // 2 - 1 - (pair >> 1)) * (1 - 2 * (slot & 1))
+        ahead = jnp.where(slot == RINGS - 2, RINGS // 2, jnp.where(slot == RINGS - 1, 0, ahead))
         return ((((z + RINGS - ahead) & 15) * PLANE) + ((k >> 5) & 7)) * 4 + (k & 3)
 
     spread[...] = one_hot(station, 1, (STATIONS, ROWS))
@@ -333,8 +338,7 @@
             y = jnp.where(left, powers[0], powers[1]).astype(bf16)
             share[t] = y.reshape(RINGS, DESKS, LANES)
 
-            def send_a_step(i, _, t=t):
-                zz = (z + i) % RINGS
+            def send_a_one(zz):
                 pltpu.make_async_remote_copy(
                     src_ref=share.at[t, zz],
                     dst_ref=share_in.at[t, slot],
@@ -343,9 +347,14 @@
                     device_id=(band, zz * PLANE + j),
                     device_id_type=MESH,
                 ).start()
+
+            def send_a_two(h, _):
+                for way in (band % 2, (band + 1) % 2):
+                    send_a_one((z + distance(h) * (1 - 2 * way) + RINGS) % RINGS)
                 return 0
 
-            lax.fori_loop(1, RINGS, send_a_step, 0)
+            send_a_one((z + RINGS // 2) % RINGS)
+            lax.fori_loop(0, RINGS // 2 - 1, send_a_two, 0)
             pltpu.make_async_copy(share.at[t, z], share_in.at[t, slot], recv_a.at[t]).start()
 
     for group in range(4):

time: 87.6 us -> 86.6 us (0.989)
  Pallas kernels: 85.4 us -> 84.4 us
    pallas_call x1, Pallas kernels: 85.4 us -> 84.4 us  [local(): pl.pallas_call(kernel, name='beams', out_shape=jax.ShapeDtypeStruct((FRAM...]
where the time goes in v4:
time: 86.6 us; the launch traced here: 86.4 us
  Pallas kernels  84.4 us (97%)
  local copies, waits for them, and re-layouts  1.99 us (2%)
    pallas_call x1, Pallas kernels, local(): pl.pallas_call(kernel, name='beams', out_shape=jax.ShapeDtypeStruct((FRAM...  84.4 us
    reshape x1, local copies, waits for them, and re-layouts, local(): return formed.reshape(1, FRAMES, BANDS * CHANS * KEEP)  1.99 us

profile of v4, /device:TPU:1, one launch (start us, length us, event | category | flops | bytes accessed | tf_op | source)
XLA Modules:
  0.0 86.4 jit_solution(13025296000063142412)
XLA Ops:
  0.0 84.4 %beams.1 = bf16[3,4,16,576]{3,2,1,0:T(8,128)(2,1)} custom-call(bf16[2,4,2,48,1408]{4,3,2,1,0:T(8,128)(2,1)} %volts.1, f32[4,640]{1,0:T(4,128)} %constant.4.clone.taper, f32[256,768]{1,0:T(8,128)} %constant.5.clone.waves_far, s32[1,512]{1,0:T(1,128)} %bitcast.3, s32[512,512]{1,0:T(8,128)} %delays.1), custom_call_target="tpu_custom_call" | custom-call | tf_op jit(solution)/shard_map/beams/pallas_call | solution.py:435
  84.4 2.0 %reshape.7 = bf16[1,3,36864]{2,1,0:T(4,128)(2,1)} reshape(bf16[3,4,16,576]{3,2,1,0:T(8,128)(2,1)} %beams.1) | data formatting | bytes 442368 | tf_op jit(solution)/shard_map/reshape | solution.py:469

commit v5 on v4

--- a/solution.py
+++ b/solution.py
@@ -298,8 +298,6 @@
     for group in range(4):
         lax.fori_loop(group * 8, group * 8 + 8, weight_step, 0)
         pass_group(0, group)
-    pass_group(1, 0)
-    pass_group(1, 1)
 
     upper = lax.broadcasted_iota(jnp.int32, (1, 8, LANES), 1) < 4
     sign = jnp.where(upper, 1.0, -1.0)
@@ -360,8 +358,10 @@
     for group in range(4):
         gather(0, group)
     form(0)
+    pass_group(1, 0)
+    pass_group(1, 1)
+    gather(1, 0)
     pass_group(1, 2)
-    gather(1, 0)
     gather(1, 1)
     pass_group(1, 3)
     gather(1, 2)

time: 86.6 us -> 86.7 us (level)
  no operation moved by 1% of the time
where the time goes in v5:
time: 86.7 us; the launch traced here: 86.5 us
  Pallas kernels  84.5 us (97%)
  local copies, waits for them, and re-layouts  1.99 us (2%)
    pallas_call x1, Pallas kernels, local(): pl.pallas_call(kernel, name='beams', out_shape=jax.ShapeDtypeStruct((FRAM...  84.5 us
    reshape x1, local copies, waits for them, and re-layouts, local(): return formed.reshape(1, FRAMES, BANDS * CHANS * KEEP)  1.99 us

profile of v5, /device:TPU:1, one launch (start us, length us, event | category | flops | bytes accessed | tf_op | source)
XLA Modules:
  0.0 86.5 jit_solution(563380792181510579)
XLA Ops:
  0.0 84.5 %beams.1 = bf16[3,4,16,576]{3,2,1,0:T(8,128)(2,1)} custom-call(bf16[2,4,2,48,1408]{4,3,2,1,0:T(8,128)(2,1)} %volts.1, f32[4,640]{1,0:T(4,128)} %constant.4.clone.taper, f32[256,768]{1,0:T(8,128)} %constant.5.clone.waves_far, s32[1,512]{1,0:T(1,128)} %bitcast.3, s32[512,512]{1,0:T(8,128)} %delays.1), custom_call_target="tpu_custom_call" | custom-call | tf_op jit(solution)/shard_map/beams/pallas_call | solution.py:435
  84.5 2.0 %reshape.7 = bf16[1,3,36864]{2,1,0:T(4,128)(2,1)} reshape(bf16[3,4,16,576]{3,2,1,0:T(8,128)(2,1)} %beams.1) | data formatting | bytes 442368 | tf_op jit(solution)/shard_map/reshape | solution.py:469
